TPU v7x, 32 devices: a whole 2x2x4 slice. The times are simulated.
32 devices in a mesh: dp: 8 (over y, x, core), tensor: 4 (over z).
Axes of the slice: x: 2, y: 2, z: 4, core: 2. Of those that a mesh axis runs over, the one named last changes fastest.
Arguments:
- tokens: bfloat16 [1024, 8, 1024], P('tensor', 'dp'), may hold values from -6 to 6
- cotangent: bfloat16 [1024, 8, 1024], P('tensor', 'dp'), may hold values from -6 to 6
- clip_mask: int32 [8], P('dp'), may hold values from 0 to 1, as said below
- positions: int32 [3, 8, 1024], P(None, 'dp'), may hold values from 0 to 15
- triple_weight: bfloat16 [2, 1024, 3, 1024], P(None, 'dp', None, 'tensor'), may hold values from -0.1875 to 0.1875
- triple_bias: bfloat16 [2, 3, 1024], P(None, None, 'tensor'), may hold values from -0.75 to 0.75
- exit_weight: bfloat16 [2, 1024, 1024], P(None, 'tensor', 'dp'), may hold values from -2 to 2
- expand_weight: bfloat16 [2, 1024, 4096], P(None, 'dp', 'tensor'), may hold values from -0.1875 to 0.1875
- expand_bias: bfloat16 [2, 4096], P(None, 'tensor'), may hold values from -4 to 4
- shrink_weight: bfloat16 [2, 4096, 1024], P(None, 'tensor', 'dp'), may hold values from -0.09375 to 0.09375
- norm_gain: bfloat16 [2, 2, 1024], replicated, may hold values from 0.5 to 1.5
- norm_shift: bfloat16 [2, 2, 1024], replicated, may hold values from -3 to 3
- branch_bias: bfloat16 [2, 2, 1024], replicated, may hold values from -4 to 4
Outputs:
- mixed: float32 [1024, 8, 1024], P('tensor', 'dp')
- tokens_gradient: float32 [1024, 8, 1024], P('tensor', 'dp')
- triple_gradient: float32 [2, 1024, 3, 1024], P(None, 'dp', None, 'tensor')
- triple_bias_gradient: float32 [2, 3, 1024], P(None, None, 'tensor')
- exit_gradient: float32 [2, 1024, 1024], P(None, 'tensor', 'dp')
- expand_gradient: float32 [2, 1024, 4096], P(None, 'dp', 'tensor')
- expand_bias_gradient: float32 [2, 4096], P(None, 'tensor')
- shrink_gradient: float32 [2, 4096, 1024], P(None, 'tensor', 'dp')
- gain_gradient: float32 [2, 2, 1024], replicated
- shift_gradient: float32 [2, 2, 1024], replicated
- branch_bias_gradient: float32 [2, 2, 1024], replicated
Inputs may be any that keep to these rules, and one draw needn't show every extreme that they name: `clip_mask`: exactly 1 of the 8 slots hold 0.
All inputs are finite; a program needn't handle non-finite values.
Results may differ from a plain program's by a relative error of at most 0.015.
Values may be sent and summed in bfloat16 or wider, within the bound.
A program may use at most 128 MiB of HBM per device.

v0:
```python
import functools

import jax
import jax.numpy as jnp
from jax import lax
from jax.experimental import pallas as pl
from jax.experimental.pallas import tpu as pltpu
from jax.sharding import PartitionSpec as P

HEAD_DIM = 64
ROT = 20
LAYERS = 2
CHUNKS = 4
LANES = 128
EPSILON = 1e-06
LOG2E = 1.4426950408889634
LN2 = 0.6931471805599453
SCALE = HEAD_DIM ** (-0.5)
RSQRT_2PI = 0.3989422804014327
F32, BF16 = jnp.float32, jnp.bfloat16
NN = (((1,), (0,)), ((), ()))
NT = (((1,), (1,)), ((), ()))
TN = (((0,), (0,)), ((), ()))
MESH = pl.DeviceIdType.MESH
ANY = pl.BlockSpec(memory_space=pl.ANY)
VMEM = pl.BlockSpec(memory_space=pltpu.VMEM)
VMEM_LIMIT = 59 * 2**20


def dot(left, right, dims):
    return lax.dot_general(left, right, dims, preferred_element_type=F32)


def tile(index, size):
    return pl.ds(pl.multiple_of(index * size, size), size)


class Place:
    def __init__(self):
        self.dh, self.b, self.th, self.tl = [lax.axis_index(a) for a in ("dh", "b", "th", "tl")]
        self.n = lax.axis_size("dh")
        self.me = (self.dh, self.b, self.th, self.tl)
        self.sib = (self.dh, 1 - self.b, self.th, self.tl)
        self.link = (self.dh, self.b, self.th, 1 - self.tl)
        self.other = (self.dh, self.th, self.b, self.tl)
        self.mine = 2 * self.b + self.tl
        self.links = 2 * self.b + 1 - self.tl
        self.sibs = 2 * (1 - self.b) + self.tl
        self.diags = 2 * (1 - self.b) + 1 - self.tl

    def turn(self, which):
        y, x = self.dh // 2, lax.rem(self.dh, 2)
        across, along = 2 * y + 1 - x, 2 * (1 - y) + x
        first = self.b if which else 1 - self.b
        return first * across + (1 - first) * along

    def opposite(self):
        y, x = self.dh // 2, lax.rem(self.dh, 2)
        return 2 * (1 - y) + 1 - x

    def near(self, dh):
        return (dh, self.b, self.th, self.tl)

    def peer(self, step):
        return (lax.rem(self.dh + step, self.n), self.b, self.th, self.tl)

    def barrier(self):
        sem = pltpu.get_barrier_semaphore()
        greeted = [
            self.sib,
            self.link,
            (self.dh, self.b, 1 - self.th, self.tl),
            (self.dh, 1 - self.b, 1 - self.th, self.tl),
        ] + [self.peer(step) for step in range(1, self.n)]
        for device in greeted:
            pl.semaphore_signal(sem, inc=1, device_id=device, device_id_type=MESH)
        pl.semaphore_wait(sem, len(greeted))


def remote(src, dst, send, recv, device):
    return pltpu.make_async_remote_copy(
        src_ref=src, dst_ref=dst, send_sem=send, recv_sem=recv, device_id=device, device_id_type=MESH
    )


class Swap:
    def __init__(self, at, src, dst, sems):
        self.same = at.b == at.th
        self.far = remote(src, dst, sems.at[0], sems.at[1], at.other)
        self.near = pltpu.make_async_copy(src, dst, sems.at[2])

    def start(self):
        pl.when(self.same)(self.near.start)
        pl.when(jnp.logical_not(self.same))(self.far.start)

    def wait(self):
        pl.when(self.same)(self.near.wait)
        pl.when(jnp.logical_not(self.same))(self.far.wait)


class Gather:
    def __init__(self, at, src, full, zsems, psems):
        self.at, self.src, self.full = at, src, full
        self.zsems, self.psems = zsems, psems
        self.size = src.shape[0]
        self.same = at.b == at.th

    def slot(self, b):
        return self.full.at[tile(self.at.dh * 2 + b, self.size)]

    def block(self, dh):
        return self.full.at[tile(dh, 2 * self.size)]

    def zcopies(self):
        at = self.at
        dst = self.slot(at.b)
        far = remote(
            self.src,
            dst,
            self.zsems.at[0],
            self.zsems.at[4 + at.b],
            (at.dh, at.th, 1 - at.th, at.tl),
        )
        near = remote(self.src, dst, self.zsems.at[1], self.zsems.at[3], at.sib)
        own = pltpu.make_async_copy(self.src, dst, self.zsems.at[2])
        return far, near, own

    def zstart(self):
        far, near, own = self.zcopies()
        far.start()
        pl.when(self.same)(own.start)
        pl.when(jnp.logical_not(self.same))(near.start)

    def arrival(self, b, sem):
        return remote(self.src, self.slot(b), self.zsems.at[0], self.zsems.at[sem], self.at.sib)

    def zwait(self):
        at = self.at
        far, near, own = self.zcopies()
        far.wait_send()

        @pl.when(self.same)
        def _():
            own.wait()
            self.arrival(1 - at.b, 3).wait_recv()

        @pl.when(jnp.logical_not(self.same))
        def _():
            near.wait_send()
            self.arrival(at.b, 4 + at.b).wait_recv()
            self.arrival(1 - at.b, 5 - at.b).wait_recv()

    def pcopy(self, step, dh, device):
        block = self.block(dh)
        return remote(
            block, block, self.psems.at[0, step], self.psems.at[1, step], self.at.near(device)
        )

    def hop(self, which, dh):
        return self.pcopy(which, dh, self.at.turn(which % 2))

    def pstart(self):
        at = self.at
        if at.n == 4:
            self.hop(0, at.dh).start()
            self.hop(1, at.dh).start()
        else:
            for step in range(1, at.n):
                self.pcopy(step, at.dh, lax.rem(at.dh + step, at.n)).start()

    def pforward(self):
        if self.at.n == 4:
            first = self.at.turn(0)
            self.hop(0, first).wait_recv()
            self.pcopy(2, first, self.at.turn(1)).start()

    def pwait(self):
        at = self.at
        if at.n == 4:
            self.hop(0, at.dh).wait_send()
            self.hop(1, at.dh).wait_send()
            self.pcopy(2, at.turn(0), at.turn(1)).wait_send()
            self.hop(1, at.turn(1)).wait_recv()
            self.pcopy(2, at.opposite(), at.turn(1)).wait_recv()
        else:
            for step in range(1, at.n):
                source = lax.rem(at.dh + at.n - step, at.n)
                self.pcopy(step, at.dh, source).wait_send()
                self.pcopy(step, source, source).wait_recv()

    @staticmethod
    def scratch(n):
        return [pltpu.SemaphoreType.DMA((6,)), pltpu.SemaphoreType.DMA((2, n))]


class Scatter:
    def __init__(self, at, grad, out, flip, got, mid, zgot, psems, zsems):
        self.at, self.grad, self.out, self.flip = at, grad, out, flip
        self.got, self.mid, self.zgot = got, mid, zgot
        self.psems, self.zsems = psems, zsems
        self.size = mid.shape[0] // 2
        self.same = at.b == at.th

    @staticmethod
    def scratch(n, rows, columns):
        size = rows // n
        return [
            pltpu.VMEM((n - 1, size, columns), BF16),
            pltpu.VMEM((size, columns), BF16),
        ]

    @staticmethod
    def layer_scratch(n, rows, columns):
        return [
            pltpu.VMEM((2, rows // n // 2, columns), BF16),
            pltpu.SemaphoreType.DMA((2, n)),
            pltpu.SemaphoreType.DMA((6,)),
        ]

    def part(self, dh):
        return self.grad.at[tile(dh, 2 * self.size)]

    def pcopy(self, step, src, device):
        return remote(
            src,
            self.got.at[step],
            self.psems.at[0, step],
            self.psems.at[1, step],
            self.at.near(device),
        )

    def hop(self, index):
        at = self.at
        if index == 2:
            return self.pcopy(2, self.mid, at.turn(1))
        return self.pcopy(index, self.part(at.opposite() if index else at.turn(0)), at.turn(0))

    def pstart(self):
        at = self.at
        if at.n == 4:
            self.hop(1).start()
            self.hop(0).start()
        else:
            for step in range(1, at.n):
                target = lax.rem(at.dh + step, at.n)
                self.pcopy(step - 1, self.part(target), target).start()

    def pforward(self):
        at = self.at
        if at.n == 4:
            self.hop(1).wait()
            total = self.grad[tile(at.turn(1), 2 * self.size), :].astype(F32)
            self.mid[...] = (total + self.got[1].astype(F32)).astype(BF16)
            self.hop(2).start()

    def psum(self):
        at = self.at
        total = self.grad[tile(at.dh, 2 * self.size), :].astype(F32)
        if at.n == 4:
            self.hop(0).wait()
            self.hop(2).wait()
            total = total + self.got[0].astype(F32) + self.got[2].astype(F32)
        else:
            for step in range(1, at.n):
                target = lax.rem(at.dh + step, at.n)
                self.pcopy(step - 1, self.part(target), target).wait()
                total = total + self.got[step - 1].astype(F32)
        self.mid[...] = total.astype(BF16)

    def piece(self, b):
        return self.mid.at[tile(b, self.size)]

    def zcopies(self):
        at, sems = self.at, self.zsems
        dst = self.zgot.at[at.th]
        own = pltpu.make_async_copy(self.piece(at.b), dst, sems.at[0])
        near = remote(self.piece(1 - at.b), dst, sems.at[1], sems.at[4], at.sib)
        first = remote(
            self.piece(at.b), dst, sems.at[2], sems.at[5], (at.dh, at.b, 1 - at.th, at.tl)
        )
        second = remote(
            self.piece(1 - at.b), dst, sems.at[3], sems.at[5], (at.dh, 1 - at.b, 1 - at.th, at.tl)
        )
        return own, near, first, second

    def zstart(self):
        own, near, first, second = self.zcopies()

        @pl.when(self.same)
        def _():
            near.start()
            own.start()

        @pl.when(jnp.logical_not(self.same))
        def _():
            first.start()
            second.start()

    def arrival(self, th, sem):
        return remote(
            self.piece(0), self.zgot.at[th], self.zsems.at[0], self.zsems.at[sem], self.at.sib
        )

    def zsum(self):
        at = self.at
        own, near, first, second = self.zcopies()

        @pl.when(self.same)
        def _():
            near.wait_send()
            own.wait()

        @pl.when(jnp.logical_not(self.same))
        def _():
            first.wait_send()
            second.wait_send()
            self.arrival(at.th, 4).wait_recv()

        self.arrival(1 - at.th, 5).wait_recv()
        total = self.zgot[0].astype(F32) + self.zgot[1].astype(F32)
        self.out[...] = total.T if self.flip else total


class Rows:
    def __init__(self, at, count):
        self.at, self.R = at, count // CHUNKS

    def at_(self, chunk, owner):
        return tile(chunk * 4 + owner, self.R)

    def whole(self, chunk):
        return pl.ds(chunk * 4 * self.R, 4 * self.R)

    def own(self, chunk):
        return pl.ds(chunk * self.R, self.R)


class Spread:
    def __init__(self, at, rows, buf, sems):
        self.at, self.rows, self.buf, self.sems = at, rows, buf, sems

    @staticmethod
    def scratch(width):
        return [pltpu.SemaphoreType.DMA((6, CHUNKS))]

    def copy(self, chunk, kind, owner):
        ref = self.buf.at[self.rows.at_(chunk, owner)]
        device = self.at.link if kind == 0 else self.at.sib
        return remote(ref, ref, self.sems.at[kind, chunk], self.sems.at[3 + kind, chunk], device)

    def start(self, chunk):
        self.copy(chunk, 0, self.at.mine).start()
        self.copy(chunk, 1, self.at.mine).start()

    def forward(self, chunk):
        self.copy(chunk, 0, self.at.links).wait_recv()
        self.copy(chunk, 2, self.at.links).start()

    def wait(self, chunk):
        self.copy(chunk, 1, self.at.sibs).wait_recv()
        self.copy(chunk, 2, self.at.diags).wait_recv()

    def finish(self):
        for chunk in range(CHUNKS):
            self.copy(chunk, 0, self.at.mine).wait_send()
            self.copy(chunk, 1, self.at.mine).wait_send()
            self.copy(chunk, 2, self.at.links).wait_send()


class Collect:
    def __init__(self, at, rows, part, sent, got, sent_far, got_far, sems):
        self.at, self.R, self.part = at, rows.R, part
        self.sent, self.got, self.sent_far, self.got_far, self.sems = sent, got, sent_far, got_far, sems

    @staticmethod
    def scratch(count, width):
        R = count // CHUNKS
        return [
            pltpu.VMEM((CHUNKS, 2 * R, width), BF16),
            pltpu.VMEM((CHUNKS, 2 * R, width), BF16),
            pltpu.VMEM((CHUNKS, R, width), BF16),
            pltpu.VMEM((CHUNKS, R, width), BF16),
        ]

    SEMS = pltpu.SemaphoreType.DMA((4, CHUNKS))

    def near(self, chunk):
        return remote(
            self.sent.at[chunk],
            self.got.at[chunk],
            self.sems.at[0, chunk],
            self.sems.at[1, chunk],
            self.at.sib,
        )

    def far(self, chunk):
        return remote(
            self.sent_far.at[chunk],
            self.got_far.at[chunk],
            self.sems.at[2, chunk],
            self.sems.at[3, chunk],
            self.at.link,
        )

    def left(self, ref, chunk):
        halves = [ref[tile(2 * chunk + b, 2 * self.R), :] for b in (self.at.b, 1 - self.at.b)]
        return jnp.concatenate(halves, axis=0)

    def put(self, chunk, span, values):
        self.part[chunk, :, span] = values[: 2 * self.R]
        self.sent[chunk, :, span] = values[2 * self.R :].astype(BF16)

    def start(self, chunk):
        self.near(chunk).start()

    def half(self, chunk, tl):
        mine = self.part[chunk, tile(tl, self.R), :]
        return mine + self.got[chunk, tile(tl, self.R), :].astype(F32)

    def forward(self, chunk):
        self.near(chunk).wait_recv()
        self.sent_far[chunk] = self.half(chunk, 1 - self.at.tl).astype(BF16)
        self.far(chunk).start()

    def take(self, chunk):
        self.far(chunk).wait_recv()
        return self.half(chunk, self.at.tl) + self.got_far[chunk].astype(F32)

    def finish(self):
        for chunk in range(CHUNKS):
            self.near(chunk).wait_send()
            self.far(chunk).wait_send()


class Take:
    def __init__(self, refs):
        self.refs = list(refs)

    def __call__(self, count=None):
        if count is None:
            return self.refs.pop(0)
        return [self.refs.pop(0) for _ in range(count)]


class Local:
    def __init__(self, sems):
        self.sems, self.used = sems, 0

    def start(self, src, dst):
        copy = pltpu.make_async_copy(src, dst, self.sems.at[self.used])
        self.used += 1
        copy.start()
        return copy


def stats(values):
    center = values - jnp.mean(values, axis=-1, keepdims=True)
    inverse = lax.rsqrt(jnp.mean(center * center, axis=-1, keepdims=True) + EPSILON)
    return center * inverse, inverse


def norm(values, gain, shift):
    return stats(values)[0] * gain + shift


def norm_back(upstream, scaled, inverse, gain):
    weighted = upstream * gain
    first_mean = jnp.mean(weighted, axis=-1, keepdims=True)
    second_mean = jnp.mean(weighted * scaled, axis=-1, keepdims=True)
    return inverse * (weighted - first_mean - scaled * second_mean)


def lane():
    return lax.broadcasted_iota(jnp.int32, (1, LANES), 1)


def turned(values, cosines, sines):
    within = lax.rem(lane(), HEAD_DIM)
    former = lax.rem(within, ROT) < ROT // 2
    half = ROT // 2
    moved = jnp.where(former, pltpu.roll(values, LANES - half, 1), pltpu.roll(values, half, 1))
    return values * cosines + moved * sines


def of_head(values, head):
    keep = (lane() // HEAD_DIM) == head % 2
    return jnp.where(keep, values, jnp.zeros_like(values))


def gelu_and_slope(u):
    size = jnp.abs(u) * 0.7071067811865476
    t = 1.0 / (1.0 + 0.3275911 * size)
    bell = jnp.exp(-0.5 * u * u)
    poly = t * (
        0.127414796
        + t * (-0.142248368 + t * (0.7107068705 + t * (-0.7265760135 + t * 0.5307027145)))
    )
    tail = poly * bell
    phi = jnp.where(u < 0, tail, 1.0 - tail)
    return u * phi, phi + u * bell * RSQRT_2PI


def tables(places, cosines, sines, rows):
    row = lax.broadcasted_iota(jnp.int32, (HEAD_DIM, places.shape[1]), 0)
    which = row // ROT
    place = jnp.where(
        which == 0, places[0:1, :], jnp.where(which == 1, places[1:2, :], places[2:3, :])
    )
    step = lax.rem(row, ROT // 2).astype(F32) / (ROT // 2)
    frequency = jnp.where(which < 3, jnp.exp(step * -9.210340371976184), 0.0)
    angle = place * frequency
    sign = jnp.where(lax.rem(row, ROT) < ROT // 2, -1.0, 1.0)
    for table, values in ((cosines, jnp.cos(angle)), (sines, jnp.sin(angle) * sign)):
        turned_values = jnp.concatenate([values, values], axis=0).T
        for k in range(CHUNKS):
            for owner in range(4):
                start = (owner * CHUNKS + k) * rows.R
                table[pl.ds((k * 4 + owner) * rows.R, rows.R), :] = turned_values[
                    start : start + rows.R, :
                ]


def forward_kernel(n, refs):
    take = Take(refs)
    tokens, cotangent, clip_mask, positions = take(4)
    triple_in, triple_bias, exit_in, expand_in, expand_bias, shrink_in = take(6)
    norm_gain, norm_shift, branch_bias = take(3)
    mixed, upstream, cosines_out, sines_out = take(4)
    outs = [take(15) for _ in range(LAYERS)]
    x, smalls, small, parameters, turned_tokens, turned_cotangent, cosines, sines = take(8)
    exit_turned, shrink_turned = take(2)
    weights = [take(4) for _ in range(LAYERS)]
    n1, n2, qp, kp, vp, vt, o, g, slope, lse, ot, part = take(12)
    spread_sems = take(2 * LAYERS)
    one_buffers, two_buffers = take(4), take(4)
    collect_sems = take(2 * LAYERS)
    gather_sems = [[take(2) for _ in range(4)] for _ in range(LAYERS)]
    token_sems, small_sems, cotangent_sems, local_sems = take(4)

    at = Place()
    local = Local(local_sems)
    rows = Rows(at, x.shape[0])
    slices = [
        [source.at[l] for source in (triple_in, exit_turned, expand_in, shrink_turned)]
        for l in range(LAYERS)
    ]
    gathers = [
        [Gather(at, *triple) for triple in zip(slices[l], weights[l], *zip(*gather_sems[l]))]
        for l in range(LAYERS)
    ]
    smalls[...] = jnp.zeros_like(smalls)
    smalls[0:3, :] = positions[...].astype(F32)
    smalls[3:4, :] = jnp.broadcast_to(clip_mask[...].astype(F32), (1, smalls.shape[1]))
    for l in range(LAYERS):
        for kind in range(3):
            width = triple_bias.shape[2]
            smalls[4 + l : 5 + l, kind * width : (kind + 1) * width] = triple_bias[
                l, kind : kind + 1, :
            ].astype(F32)
        smalls[6 + l : 7 + l, :] = expand_bias[l : l + 1, :].astype(F32)
    swap_small = Swap(at, smalls, small, small_sems)
    swap_tokens = [
        Swap(
            at,
            tokens.at[rows.own(k)],
            turned_tokens.at[rows.own(k)],
            token_sems.at[k],
        )
        for k in range(CHUNKS)
    ]
    swap_cotangent = Swap(at, cotangent, turned_cotangent, cotangent_sems)

    at.barrier()
    gathers[0][0].zstart()
    swap_small.start()
    for swap in swap_tokens:
        swap.start()
    for l in range(LAYERS):
        exit_turned[l] = exit_in[l].T
        shrink_turned[l] = shrink_in[l].T
        for index, source in enumerate((norm_gain, norm_shift, branch_bias)):
            parameters[8 * l + 2 * index : 8 * l + 2 * index + 2, :] = source[l].astype(F32)
    swap_small.wait()
    tables(small, cosines, sines, rows)
    saves = [local.start(cosines, cosines_out), local.start(sines, sines_out)]

    def begin(l):
        spread = [Spread(at, rows, buf, spread_sems[2 * l + i]) for i, buf in enumerate((n1, n2))]
        collect = [
            Collect(at, rows, part, *buffers, collect_sems[2 * l + i])
            for i, buffers in enumerate((one_buffers, two_buffers))
        ]
        return spread + collect

    stages = [begin(l) for l in range(LAYERS)]

    def row(l, index):
        return parameters[8 * l + index : 8 * l + index + 1, :]

    def first_norm(l, k):
        n1[rows.at_(k, at.mine), :] = norm(x[rows.own(k), :], row(l, 0), row(l, 2)).astype(BF16)
        stages[l][0].start(k)

    def project(l, k):
        stages[l][0].wait(k)
        whole = rows.whole(k)
        wa = weights[l][0]
        for kind in range(3):
            columns = slice(2 * kind * LANES, 2 * (kind + 1) * LANES)
            bias = small[4 + l : 5 + l, columns]
            both = dot(n1[whole, :], wa[:, columns], NN) + bias
            for pair in range(2):
                t = both[:, pair * LANES : (pair + 1) * LANES]
                if kind < 2:
                    t = turned(t, cosines[whole, :], sines[whole, :])
                if kind == 0:
                    qp[pair, whole, :] = (t * (SCALE * LOG2E)).astype(BF16)
                elif kind == 1:
                    kp[pair, whole, :] = t.astype(BF16)
                else:
                    vp[pair, whole, :] = t.astype(BF16)
                    vt[pl.ds(pair * LANES, LANES), whole] = t.T.astype(BF16)

    def attention(k):
        whole = rows.whole(k)

        def head(h, carry):
            scores = dot(kp[h // 2], of_head(qp[h // 2, whole, :], h), NT)
            highest = jnp.max(scores, axis=0, keepdims=True)
            weights = jnp.exp2(scores - highest)
            total = jnp.sum(weights, axis=0, keepdims=True)
            spans = tile(h, HEAD_DIM)
            ot[spans, :] = dot(vt[spans, :], weights.astype(BF16), NN) / total
            lse[pl.ds(h, 1), whole] = highest + jnp.log2(total)
            return carry

        lax.fori_loop(0, 4, head, 0)
        o[whole, :] = ot[...].T.astype(BF16)

    def leave(l, k):
        wb, collect = weights[l][1], stages[l][2]
        left = collect.left(o, k)

        def columns(j, carry):
            span = tile(j, 256)
            collect.put(k, span, dot(left, wb[span, :], NT))
            return carry

        lax.fori_loop(0, part.shape[2] // 256, columns, 0)
        collect.start(k)

    def second_norm(l, k):
        own = rows.own(k)
        x[own, :] = x[own, :] + (stages[l][2].take(k) + row(l, 4))
        n2[rows.at_(k, at.mine), :] = norm(x[own, :], row(l, 1), row(l, 3)).astype(BF16)
        stages[l][1].start(k)

    def up(l, k):
        whole = rows.whole(k)
        wc = weights[l][2]
        stages[l][1].wait(k)

        def columns(j, carry):
            span = tile(j, 256)
            u = dot(n2[whole, :], wc[:, span], NN) + small[pl.ds(6 + l, 1), span]
            active, grade = gelu_and_slope(u)
            g[whole, span] = active.astype(BF16)
            slope[whole, span] = grade.astype(BF16)
            return carry

        lax.fori_loop(0, wc.shape[1] // 256, columns, 0)

    def down(l, k):
        wd, collect = weights[l][3], stages[l][3]
        left = collect.left(g, k)

        def outputs(j, carry):
            span = tile(j, 256)
            collect.put(k, span, dot(left, wd[span, :], NT))
            return carry

        lax.fori_loop(0, part.shape[2] // 256, outputs, 0)
        collect.start(k)

    def end(l, k):
        own = rows.own(k)
        x[own, :] = x[own, :] + (stages[l][3].take(k) + row(l, 5))
        if l + 1 < LAYERS:
            first_norm(l + 1, k)

    A, B, C, D = range(4)

    def begin_plane(gather):
        gather.zwait()
        gather.pstart()

    begin_plane(gathers[0][A])
    for k in range(CHUNKS):
        swap_tokens[k].wait()
        x[rows.own(k), :] = turned_tokens[rows.own(k), :].astype(F32)
        first_norm(0, k)
    for gather in gathers[0][B:]:
        gather.zstart()
    gathers[0][A].pforward()
    pending = []
    for l in range(LAYERS):
        hidden_out, middle_out, *full_outs = outs[l][:6]
        n1_out, n2_out, qp_out, kp_out, vp_out, o_out, g_out, slope_out, lse_out = outs[l][6:]
        spread_one, spread_two, collect_one, collect_two = stages[l]
        now = gathers[l]
        following = gathers[l + 1] if l + 1 < LAYERS else None
        save_x = local.start(x, hidden_out)
        for k in range(CHUNKS):
            spread_one.forward(k)
        now[A].pwait()
        if l == 0:
            begin_plane(now[B])
        else:
            now[B].pforward()
            begin_plane(now[C])
        for save in pending:
            save.wait()
        for k in range(CHUNKS):
            project(l, k)
        spread_one.finish()
        save_n1 = local.start(n1, n1_out)
        pending = [
            local.start(*pair) for pair in ((qp, qp_out), (kp, kp_out), (vp, vp_out))
        ]
        if l == 0:
            now[B].pforward()
        attention(0)
        now[B].pwait()
        leave(l, 0)
        if l == 0:
            begin_plane(now[C])
        attention(1)
        collect_one.forward(0)
        leave(l, 1)
        if l:
            begin_plane(now[D])
            now[C].pforward()
        save_x.wait()
        attention(2)
        collect_one.forward(1)
        leave(l, 2)
        second_norm(l, 0)
        attention(3)
        collect_one.forward(2)
        leave(l, 3)
        if l == 0:
            now[C].pforward()
            begin_plane(now[D])
        second_norm(l, 1)
        collect_one.forward(3)
        second_norm(l, 2)
        second_norm(l, 3)
        if following:
            following[A].zstart()
            following[B].zstart()
        save_x = local.start(x, middle_out)
        pending += [local.start(o, o_out), local.start(lse, lse_out)]
        save_n1.wait()
        spread_two.forward(0)
        now[C].pwait()
        for k in range(CHUNKS):
            up(l, k)
            if k == 1:
                now[D].pforward()
            if k + 1 < CHUNKS:
                spread_two.forward(k + 1)
        save_x.wait()
        spread_two.finish()
        now[D].pwait()
        for k in range(CHUNKS):
            down(l, k)
            if k:
                collect_two.forward(k - 1)
            if following:
                if k == 0:
                    begin_plane(following[A])
                    following[C].zstart()
                if k == 2:
                    begin_plane(following[B])
            if k > 1:
                end(l, k - 2)
        collect_two.forward(CHUNKS - 1)
        pending += [local.start(*pair) for pair in ((n2, n2_out), (g, g_out), (slope, slope_out))]
        pending += [local.start(*pair) for pair in zip(weights[l], full_outs)]
        end(l, CHUNKS - 2)
        if following:
            following[A].pforward()
        end(l, CHUNKS - 1)
        if following:
            following[D].zstart()
        else:
            swap_cotangent.start()
        collect_one.finish()
        collect_two.finish()
    live = small[3:4, :]
    mixed[...] = (x[...] * live).astype(BF16)
    swap_cotangent.wait()
    upstream[...] = turned_cotangent[...].astype(F32) * live
    for save in saves + pending:
        save.wait()


def backward_kernel(n, refs):
    take = Take(refs)
    upstream, mixed, gain_in = take(3)
    ins = [take(15) for _ in range(LAYERS)]
    cosines_in, sines_in = take(2)
    mixed_out, grad_out, triple_out, triple_bias_out, exit_out, expand_out = take(6)
    expand_bias_out, shrink_out, gain_out, shift_out, bias_out = take(5)
    e, xs, wa, wb, wc, wd = take(6)
    em, ea, n2, qp, kp, vp, kt, o, g, du, lse = take(11)
    dk, dv, dqt, dt, part, gd, ge, gt, vectors, cosines, sines = take(11)
    turned_mixed, low_grad_own, turned_grad = take(3)
    spread_sems = take(2 * LAYERS)
    one_buffers, two_buffers = take(4), take(4)
    collect_sems = take(2 * LAYERS)
    scatter_buffers = [take(2) for _ in range(4)]
    scatter_layers = [[take(3) for _ in range(4)] for _ in range(LAYERS)]
    mixed_sems, grad_sems = take(2)
    plane, column, plane_sems, column_sems = take(4)
    local_sems = take()

    at = Place()
    local = Local(local_sems)
    rows = Rows(at, e.shape[0])

    def load(l, name):
        where = {
            "hidden": (0, xs),
            "middle": (1, xs),
            "a": (2, wa),
            "b": (3, wb),
            "c": (4, wc),
            "d": (5, wd),
            "n1": (6, g),
            "n2": (7, n2),
            "q": (8, qp),
            "k": (9, kp),
            "v": (10, vp),
            "o": (11, o),
            "g": (12, g),
            "slope": (13, du),
            "lse": (14, lse),
        }
        index, target = where[name]
        loads[(l, name)] = local.start(ins[l][index], target)

    def ready(l, *names):
        for name in names:
            loads.pop((l, name)).wait()

    loads = {}
    top = LAYERS - 1
    load_e = local.start(upstream, e)
    for name in ("d", "slope", "c", "middle", "g", "n2", "b", "q", "k", "v", "o", "lse", "a"):
        load(top, name)
    load_tables = [local.start(cosines_in, cosines), local.start(sines_in, sines)]

    cubes = [(db, dth, dtl) for db in range(2) for dth in range(2) for dtl in range(2)][1:]

    def flipped(flips):
        return [jnp.abs(coordinate - flip) for coordinate, flip in zip(at.me[1:], flips)]

    barrier = pltpu.get_barrier_semaphore()
    greeted = [(at.dh, *flipped(flips)) for flips in cubes]
    greeted += [at.peer(step) for step in range(1, n)]
    for device in greeted:
        pl.semaphore_signal(barrier, inc=1, device_id=device, device_id_type=MESH)
    pl.semaphore_wait(barrier, len(greeted))

    spreads = [
        [Spread(at, rows, buf, spread_sems[2 * l + i]) for i, buf in enumerate((em, ea))]
        for l in range(LAYERS)
    ]
    collects = [
        [
            Collect(at, rows, part, *buffers, collect_sems[2 * l + i])
            for i, buffers in enumerate((one_buffers, two_buffers))
        ]
        for l in range(LAYERS)
    ]
    pieces = ((gt, triple_out, False), (ge, exit_out, True), (wd, expand_out, False), (gd, shrink_out, True))
    scatters = [
        [
            Scatter(at, grad, out.at[l], flip, *buffers, *own)
            for (grad, out, flip), buffers, own in zip(pieces, scatter_buffers, scatter_layers[l])
        ]
        for l in range(LAYERS)
    ]
    swap_mixed = Swap(at, mixed, turned_mixed, mixed_sems)
    swap_grads = [
        Swap(
            at, low_grad_own.at[rows.own(k)], turned_grad.at[rows.own(k)], grad_sems.at[k]
        )
        for k in range(CHUNKS)
    ]
    vectors[...] = jnp.zeros_like(vectors)

    def add(l, row, values):
        vectors[8 * l + row : 8 * l + row + 1, : values.shape[1]] += jnp.sum(
            values.astype(F32), axis=0, keepdims=True
        )

    def weight_grad(left, right, out):
        def block(j, carry):
            span = tile(j, 256)
            out[span, :] = dot(left[:, span], right[...], TN).astype(BF16)
            return carry

        lax.fori_loop(0, left.shape[1] // 256, block, 0)

    def send_branch(l, k):
        low = e[rows.own(k), :].astype(BF16)
        em[rows.at_(k, at.mine), :] = low
        spreads[l][0].start(k)
        add(l, 5, low)

    def shrink_back(l, k):
        spreads[l][0].wait(k)
        whole = rows.whole(k)
        collect = collects[l][0]

        def columns(j, carry):
            span = tile(j, 256)
            active_grad = dot(em[whole, :], wd[:, span], NN)
            du[whole, span] = (active_grad * du[whole, span].astype(F32)).astype(BF16)
            return carry

        lax.fori_loop(0, wd.shape[1] // 256, columns, 0)
        add(l, 6, du[whole, :])
        left = collect.left(du, k)

        def outputs(j, carry):
            span = tile(j, 256)
            collect.put(k, span, dot(left, wc[span, :], NT))
            return carry

        lax.fori_loop(0, part.shape[2] // 256, outputs, 0)
        collect.start(k)

    def norm_step(l, k, which):
        own = rows.own(k)
        scaled, inverse = stats(xs[own, :])
        grads = collects[l][1 - which].take(k)
        add(l, which, grads * scaled)
        add(l, 2 + which, grads)
        gain = gain_in[l, which : which + 1, :].astype(F32)
        e[own, :] = e[own, :] + norm_back(grads, scaled, inverse, gain)

    def middle_step(l, k):
        norm_step(l, k, 1)
        low = e[rows.own(k), :].astype(BF16)
        ea[rows.at_(k, at.mine), :] = low
        spreads[l][1].start(k)
        add(l, 4, low)

    def first_step(l, k):
        norm_step(l, k, 0)
        if l:
            send_branch(l - 1, k)
        else:
            low_grad_own[rows.own(k), :] = e[rows.own(k), :].astype(BF16)
            swap_grads[k].start()

    def attention_back(l, k):
        spreads[l][1].wait(k)
        whole = rows.whole(k)
        out_grad = dot(ea[whole, :], wb[...], NN)
        low_grad = out_grad.astype(BF16)
        product = low_grad.astype(F32) * o[whole, :].astype(F32)
        high = product.astype(BF16)
        rest = (product - high.astype(F32)).astype(BF16)
        for pair in range(2):
            lanes = slice(pair * LANES, (pair + 1) * LANES)
            dop = low_grad[:, lanes]
            for half in range(2):
                h = 2 * pair + half
                pick = jnp.broadcast_to(((lane() // HEAD_DIM) == half).astype(BF16), (8, LANES))
                center = dot(pick, high[:, lanes], NT) + dot(pick, rest[:, lanes], NT)
                qh = of_head(qp[pair, whole, :], half)
                doh = of_head(dop, half)
                scores = dot(kp[pair], qh, NT)
                chances = jnp.exp2(scores - lse[h : h + 1, whole])
                chance_grad = dot(vp[pair], doh, NT)
                score_grad = (chances * (chance_grad - center[0:1, :])).astype(BF16)
                dv[pair] += dot(chances.astype(BF16), doh, NN)
                dk[pair] += dot(score_grad, qh, NN)
                spans = slice(h * HEAD_DIM, (h + 1) * HEAD_DIM)
                dqt[spans, :] = dot(kt[spans, :], score_grad, NN)
        for pair in range(2):
            lanes = slice(pair * LANES, (pair + 1) * LANES)
            dq = dqt[lanes, :].T * SCALE
            dt[whole, lanes] = turned(dq, cosines[whole, :], -sines[whole, :]).astype(BF16)

    def projection_back(l, k):
        collect = collects[l][1]
        left = collect.left(dt, k)

        def outputs(j, carry):
            span = tile(j, 256)
            collect.put(k, span, dot(left, wa[span, :], NT))
            return carry

        lax.fori_loop(0, part.shape[2] // 256, outputs, 0)
        collect.start(k)

    load_e.wait()
    for k in range(CHUNKS):
        send_branch(top, k)
    swap_mixed.start()
    for l in reversed(range(LAYERS)):
        spread_one, spread_two = spreads[l]
        collect_one, collect_two = collects[l]
        st, se, sc, sd = scatters[l]
        previous = scatters[l + 1] if l < top else None
        ready(l, "d", "slope", "c", "middle")
        for k in range(CHUNKS):
            spread_one.forward(k)
            shrink_back(l, k)
            if k:
                collect_one.forward(k - 1)
            if k > 1:
                middle_step(l, k - 2)
        collect_one.forward(CHUNKS - 1)
        spread_one.finish()
        if previous:
            for scatter in previous[:2]:
                scatter.psum()
                scatter.zstart()
        ready(l, "g")
        weight_grad(em, g, gd)
        sd.pstart()
        load(l, "n1")
        middle_step(l, CHUNKS - 2)
        middle_step(l, CHUNKS - 1)
        load(l, "hidden")
        ready(l, "n2")
        weight_grad(n2, du, wd)
        sc.pstart()
        if l:
            load(l - 1, "slope")
            load(l - 1, "c")
            load(l - 1, "n2")
        ready(l, "b", "q", "k", "v", "o", "lse")
        for pair in range(2):
            kt[pl.ds(pair * LANES, LANES), :] = kp[pair].astype(F32).T.astype(BF16)
        dk[...] = jnp.zeros_like(dk)
        dv[...] = jnp.zeros_like(dv)
        if l == top:
            for copy in load_tables:
                copy.wait()
        spread_two.forward(0)
        spread_two.forward(1)
        attention_back(l, 0)
        spread_two.forward(2)
        spread_two.forward(3)
        sd.pforward()
        attention_back(l, 1)
        sc.pforward()
        attention_back(l, 2)
        if previous:
            for scatter in previous[:2]:
                scatter.zsum()
        sd.psum()
        sd.zstart()
        attention_back(l, 3)
        spread_two.finish()
        sc.psum()
        sc.zstart()
        width = 2 * LANES
        for pair in range(2):
            lanes = pl.ds(width + pair * LANES, LANES)
            dt[:, lanes] = turned(dk[pair] * LN2, cosines[...], -sines[...]).astype(BF16)
            dt[:, pl.ds(2 * width + pair * LANES, LANES)] = dv[pair].astype(BF16)
        ready(l, "a", "n1")
        weight_grad(g, dt, gt)
        st.pstart()
        for k in range(CHUNKS):
            projection_back(l, k)
            if k:
                collect_two.forward(k - 1)
        collect_two.forward(CHUNKS - 1)
        weight_grad(ea, o, ge)
        se.pstart()
        add(l, 7, dt[...])
        ready(l, "hidden")
        if l:
            for name in ("d", "g", "b", "q", "k", "v", "o", "lse", "a"):
                load(l - 1, name)
        sd.zsum()
        collect_one.finish()
        first_step(l, 0)
        first_step(l, 1)
        st.pforward()
        se.pforward()
        first_step(l, 2)
        first_step(l, 3)
        if l:
            load(l - 1, "middle")
        collect_two.finish()
        sc.zsum()

    st, se = scatters[0][:2]
    plane[at.dh] = vectors[...]

    def plane_copy(step, slot):
        ref = plane.at[slot]
        return remote(ref, ref, plane_sems.at[0, step], plane_sems.at[1, step], at.peer(step))

    for step in range(1, n):
        plane_copy(step, at.dh).start()
    for scatter in (st, se):
        scatter.psum()
        scatter.zstart()
    for step in range(1, n):
        plane_copy(step, at.dh).wait_send()
        plane_copy(step, lax.rem(at.dh + n - step, n)).wait_recv()
    total = plane[0]
    for index in range(1, n):
        total = total + plane[index]

    def slot(b, th, tl):
        return 4 * b + 2 * th + tl

    mine = slot(*at.me[1:])
    column[mine] = total

    def column_copy(index, flips, where):
        ref = column.at[where]
        device = (at.dh, *flipped(flips))
        return remote(ref, ref, column_sems.at[0, index], column_sems.at[1, index], device)

    for index, flips in enumerate(cubes):
        column_copy(index, flips, mine).start()
    swap_mixed.wait()
    mixed_out[...] = turned_mixed[...].astype(F32)
    for index, flips in enumerate(cubes):
        column_copy(index, flips, mine).wait_send()
        column_copy(index, flips, slot(*flipped(flips))).wait_recv()
    total = column[0]
    for index in range(1, 8):
        total = total + column[index]
    own = column[slot(at.th, 0, at.tl)] + column[slot(at.th, 1, at.tl)]
    width = triple_bias_out.shape[2]
    for l in range(LAYERS):
        gain_out[l] = total[8 * l : 8 * l + 2, :]
        shift_out[l] = total[8 * l + 2 : 8 * l + 4, :]
        bias_out[l] = total[8 * l + 4 : 8 * l + 6, :]
        expand_bias_out[l : l + 1, :] = own[8 * l + 6 : 8 * l + 7, :]
        for kind in range(3):
            triple_bias_out[l, kind : kind + 1, :] = own[
                8 * l + 7 : 8 * l + 8, kind * width : (kind + 1) * width
            ]
    for k in range(CHUNKS):
        swap_grads[k].wait()
    grad_out[...] = turned_grad[...].astype(F32)
    for scatter in (st, se):
        scatter.zsum()


def call(body, args, vmem_in, outs, vmem_out, scratch, collective_id, name, flops=0):
    def kernel(*refs):
        body(refs)

    in_specs = [VMEM if index in vmem_in else ANY for index in range(len(args))]
    out_specs = [VMEM if index in vmem_out else ANY for index in range(len(outs))]
    return pl.pallas_call(
        kernel,
        out_shape=outs,
        in_specs=in_specs,
        out_specs=out_specs,
        scratch_shapes=scratch,
        compiler_params=pltpu.CompilerParams(
            collective_id=collective_id, has_side_effects=True, vmem_limit_bytes=VMEM_LIMIT
        ),
        name=name,
    )(*args)


def shards(
    n,
    tokens,
    cotangent,
    clip_mask,
    positions,
    triple_weight,
    triple_bias,
    exit_weight,
    expand_weight,
    expand_bias,
    shrink_weight,
    norm_gain,
    norm_shift,
    branch_bias,
):
    count, _, depth = tokens.shape
    seq = 4 * count
    size = triple_weight.shape[1]
    local = triple_weight.shape[3]
    inner = expand_weight.shape[2]
    wide = 3 * local
    pairs = local // LANES
    R = count // CHUNKS
    V, DMA, shape = pltpu.VMEM, pltpu.SemaphoreType.DMA, jax.ShapeDtypeStruct
    wides = (wide, local, inner, inner)
    pair_shape = (pairs, seq, LANES)
    args = [
        tokens[:, 0, :],
        cotangent[:, 0, :],
        clip_mask[:, None],
        positions[:, 0, :],
        triple_weight.reshape(LAYERS, size, wide),
        triple_bias,
        exit_weight,
        expand_weight,
        expand_bias,
        shrink_weight,
        norm_gain,
        norm_shift,
        branch_bias,
    ]
    outs = [
        shape((count, depth), BF16),
        shape((count, depth), F32),
        shape((seq, LANES), F32),
        shape((seq, LANES), F32),
    ]
    for _ in range(LAYERS):
        outs += [shape((count, depth), F32)] * 2
        outs += [shape((depth, width), BF16) for width in wides]
        outs += [shape((seq, depth), BF16)] * 2
        outs += [shape(pair_shape, BF16)] * 3
        outs += [shape((seq, local), BF16)]
        outs += [shape((seq, inner), BF16)] * 2
        outs += [shape((8, seq), F32)]
    scratch = [
        V((count, depth), F32),
        V((8, depth), F32),
        V((8, depth), F32),
        V((8 * LAYERS, depth), F32),
        V((count, depth), BF16),
        V((count, depth), BF16),
        V((seq, LANES), F32),
        V((seq, LANES), F32),
        V((LAYERS, size, local), BF16),
        V((LAYERS, size, inner), BF16),
    ]
    for _ in range(LAYERS):
        scratch += [V((depth, width), BF16) for width in wides]
    scratch += [V((seq, depth), BF16)] * 2
    scratch += [V(pair_shape, BF16)] * 3
    scratch += [V((local, seq), BF16), V((seq, local), BF16)]
    scratch += [V((seq, inner), BF16)] * 2
    scratch += [V((8, seq), F32), V((local, 4 * R), F32), V((CHUNKS, 2 * R, depth), F32)]
    scratch += Spread.scratch(depth) * (2 * LAYERS)
    scratch += Collect.scratch(count, depth) * 2
    scratch += [Collect.SEMS] * (2 * LAYERS)
    scratch += Gather.scratch(n) * (4 * LAYERS)
    scratch += [DMA((CHUNKS, 3)), DMA((3,)), DMA((3,)), DMA((48,))]
    results = call(
        functools.partial(forward_kernel, n),
        args,
        tuple(range(len(args))),
        outs,
        (0, 1),
        scratch,
        1,
        "forward",
    )
    mixed, upstream, cosines, sines = results[:4]
    args = [upstream, mixed, norm_gain, *results[4:], cosines, sines]
    outs = [
        shape((count, depth), F32),
        shape((count, depth), F32),
        shape((LAYERS, size, wide), F32),
        shape(triple_bias.shape, F32),
        shape(exit_weight.shape, F32),
        shape(expand_weight.shape, F32),
        shape(expand_bias.shape, F32),
        shape(shrink_weight.shape, F32),
        shape(norm_gain.shape, F32),
        shape(norm_shift.shape, F32),
        shape(branch_bias.shape, F32),
    ]
    scratch = [V((count, depth), F32)] * 2
    scratch += [V((depth, width), BF16) for width in wides]
    scratch += [V((seq, depth), BF16)] * 3
    scratch += [V(pair_shape, BF16)] * 3
    scratch += [V((local, seq), BF16), V((seq, local), BF16)]
    scratch += [V((seq, inner), BF16)] * 2
    scratch += [V((8, seq), F32)]
    scratch += [V(pair_shape, F32)] * 2
    scratch += [V((local, 4 * R), F32), V((seq, wide), BF16), V((CHUNKS, 2 * R, depth), F32)]
    scratch += [V((depth, inner), BF16), V((depth, local), BF16), V((depth, wide), BF16)]
    scratch += [V((8 * LAYERS, depth), F32), V((seq, LANES), F32), V((seq, LANES), F32)]
    scratch += [V((count, depth), BF16)] * 3
    scratch += Spread.scratch(depth) * (2 * LAYERS)
    scratch += Collect.scratch(count, depth) * 2
    scratch += [Collect.SEMS] * (2 * LAYERS)
    for width in wides:
        scratch += Scatter.scratch(n, depth, width)
    for _ in range(LAYERS):
        for width in wides:
            scratch += Scatter.layer_scratch(n, depth, width)
    scratch += [DMA((3,)), DMA((CHUNKS, 3))]
    scratch += [V((n, 8 * LAYERS, depth), F32), V((8, 8 * LAYERS, depth), F32)]
    scratch += [DMA((2, n)), DMA((2, 7)), DMA((48,))]
    results = call(
        functools.partial(backward_kernel, n),
        args,
        (1, 2),
        outs,
        tuple(range(len(outs))),
        scratch,
        2,
        "backward",
    )
    mixed, grad, triple_total, *others = results
    return (
        mixed[:, None, :],
        grad[:, None, :],
        triple_total.reshape(triple_weight.shape),
        *others,
    )


def solution(mesh):
    n = mesh.shape["dp"] // 2
    fine = jax.sharding.Mesh(
        mesh.devices.reshape(n, 2, mesh.shape["tensor"] // 2, 2), ("dh", "b", "th", "tl")
    )
    dp, tensor = ("dh", "b"), ("th", "tl")
    return jax.shard_map(
        functools.partial(shards, n),
        mesh=fine,
        in_specs=(
            P(tensor, dp, None),
            P(tensor, dp, None),
            P(dp),
            P(None, dp, None),
            P(None, dp, None, tensor),
            P(None, None, tensor),
            P(None, tensor, dp),
            P(None, dp, tensor),
            P(None, tensor),
            P(None, tensor, dp),
            P(),
            P(),
            P(),
        ),
        out_specs=(
            P(tensor, dp, None),
            P(tensor, dp, None),
            P(None, dp, None, tensor),
            P(None, None, tensor),
            P(None, tensor, dp),
            P(None, dp, tensor),
            P(None, tensor),
            P(None, tensor, dp),
            P(),
            P(),
            P(),
        ),
        check_vma=False,
    )
```

profile of v0, /device:TPU:1, one launch (start us, length us, event | category | flops | bytes accessed | tf_op | source)
XLA Modules:
  0.0 461.2 jit_solution(2468766333786036299)
XLA Ops:
  1.3 1.3 copy.32.refs_5_
  2.6 1.3 copy.40
  3.9 1.2 copy.30
  5.1 0.9 copy.31.refs_4_
  6.0 217.5 %forward.1 = (bf16[256,1024]{1,0:T(8,128)(2,1)}, f32[256,1024]{1,0:T(8,128)}, f32[1024,128]{1,0:T(8,128)}, f32[1024,128]{1,0:T(8,128)}, f32[256,1024]{1,0:T(8,12...) custom-call(bf16[256,1024]{1,0:T(8,128)(2,1)} %bitcast.15, ...), custom_call_target="tpu_custom_call" | custom-call | tf_op jit(solution)/shard_map/forward/pallas_call | solution.py:1172
  223.5 224.8 %backward.1 = (f32[256,1024]{1,0:T(8,128)}, f32[256,1024]{1,0:T(8,128)}, f32[2,128,768]{2,1,0:T(8,128)}, f32[2,3,256]{2,1,0:T(4,128)}, f32[2,256,128]{2,1,0:T(8,...) custom-call(f32[256,1024]{1,0:T(8,128)} %get-tuple-element.56.refs_0, ...), custom_call_target="tpu_custom_call" | custom-call | tf_op jit(solution)/shard_map/backward/pallas_call | solution.py:1172
  448.3 0.0 copy-start.2
  448.3 0.0 copy-start.8
  448.3 0.0 copy-start.3
  448.3 3.4 copy.34
  451.7 0.0 copy-done.2
  451.7 2.0 copy.35
  453.8 0.0 copy-done.8
  453.8 0.0 copy-start.4
  453.8 0.0 copy-start.1
  453.8 0.6 copy.37
  454.4 0.0 copy-done.3
  454.4 0.3 copy.33
  454.7 0.0 copy-start.9
  454.7 0.0 copy-start
  454.7 1.1 copy.36
  455.8 0.0 copy-done.4
  455.8 0.7 copy.49
  456.5 0.0 copy-done.1
  456.5 0.0 copy-start.7
  456.5 0.0 copy-start.6
  456.6 0.0 copy-start.5
  456.6 1.0 copy.50
  457.5 0.0 copy-done.9
  457.5 0.6 copy.51
  458.1 0.0 copy-done
  458.1 1.0 copy.52
  459.1 0.0 copy-done.7
  459.1 0.6 copy.53
  459.7 0.0 copy-done.6
  459.7 0.6 copy.54
  460.3 0.0 copy-done.5
  460.3 0.6 copy.55
Async XLA Ops:
  448.3 3.4 copy-start.2
  448.3 5.5 %copy-start.8 = (f32[2,3,256]{2,1,0:T(4,128)S(1)}, f32[2,3,256]{2,1,0:T(4,128)}, u32[]{:S(2)}) copy-start(f32[2,3,256]{2,1,0:T(4,128)} %get-tuple-element.115) | copy-start | bytes 18436
  448.3 6.1 %copy-start.3 = (f32[2,128,768]{2,1,0:T(8,128)S(1)}, f32[2,128,768]{2,1,0:T(8,128)}, u32[]{:S(2)}) copy-start(f32[2,128,768]{2,1,0:T(8,128)} %get-tuple-element.92) | copy-start | bytes 2359300
  453.8 2.0 copy-start.4
  453.8 2.7 copy-start.1
  454.7 2.9 copy-start.9
  454.7 3.5 copy-start
  456.5 2.6 copy-start.7
  456.5 3.2 copy-start.6
  456.6 3.8 copy-start.5
where the time goes:
time: 468 us; the launch traced here: 461 us
  Pallas kernels  442 us (94%)
  local copies, waits for them, and re-layouts  17.3 us (4%)
    pallas_call x2, Pallas kernels, call(): pl.pallas_call(kernel, out_shape=outs, in_specs=in_specs, out_specs=out_s...  442 us
    unnamed x34, local copies, waits for them, and re-layouts  16.1 us

commit v1 on v0

--- a/solution.py
+++ b/solution.py
@@ -318,7 +318,11 @@
 
         self.arrival(1 - at.th, 5).wait_recv()
         total = self.zgot[0].astype(F32) + self.zgot[1].astype(F32)
-        self.out[...] = total.T if self.flip else total
+        if self.flip is None:
+            for kind in range(3):
+                self.out[kind][...] = total[:, kind * LANES : (kind + 1) * LANES]
+        else:
+            self.out[...] = total.T if self.flip else total
 
 
 class Rows:
@@ -525,23 +529,23 @@
     tokens, cotangent, clip_mask, positions = take(4)
     triple_in, triple_bias, exit_in, expand_in, expand_bias, shrink_in = take(6)
     norm_gain, norm_shift, branch_bias = take(3)
-    mixed, upstream, cosines_out, sines_out = take(4)
+    upstream, cosines_out, sines_out, small_out, em_out = take(5)
     outs = [take(15) for _ in range(LAYERS)]
     x, smalls, small, parameters, turned_tokens, turned_cotangent, cosines, sines = take(8)
-    exit_turned, shrink_turned = take(2)
+    exit_turned, shrink_turned, triple_turned, em = take(4)
     weights = [take(4) for _ in range(LAYERS)]
     n1, n2, qp, kp, vp, vt, o, g, slope, lse, ot, part = take(12)
     spread_sems = take(2 * LAYERS)
     one_buffers, two_buffers = take(4), take(4)
     collect_sems = take(2 * LAYERS)
     gather_sems = [[take(2) for _ in range(4)] for _ in range(LAYERS)]
-    token_sems, small_sems, cotangent_sems, local_sems = take(4)
+    em_sems, token_sems, small_sems, cotangent_sems, local_sems = take(5)
 
     at = Place()
     local = Local(local_sems)
     rows = Rows(at, x.shape[0])
     slices = [
-        [source.at[l] for source in (triple_in, exit_turned, expand_in, shrink_turned)]
+        [source.at[l] for source in (triple_turned, exit_turned, expand_in, shrink_turned)]
         for l in range(LAYERS)
     ]
     gathers = [
@@ -554,9 +558,9 @@
     for l in range(LAYERS):
         for kind in range(3):
             width = triple_bias.shape[2]
-            smalls[4 + l : 5 + l, kind * width : (kind + 1) * width] = triple_bias[
-                l, kind : kind + 1, :
-            ].astype(F32)
+            columns = slice(kind * width, (kind + 1) * width)
+            smalls[4 + l : 5 + l, columns] = triple_bias[kind, l : l + 1, :].astype(F32)
+            triple_turned[l, :, columns] = triple_in[l, kind]
         smalls[6 + l : 7 + l, :] = expand_bias[l : l + 1, :].astype(F32)
     swap_small = Swap(at, smalls, small, small_sems)
     swap_tokens = [
@@ -582,7 +586,11 @@
             parameters[8 * l + 2 * index : 8 * l + 2 * index + 2, :] = source[l].astype(F32)
     swap_small.wait()
     tables(small, cosines, sines, rows)
-    saves = [local.start(cosines, cosines_out), local.start(sines, sines_out)]
+    saves = [
+        local.start(*pair)
+        for pair in ((cosines, cosines_out), (sines, sines_out), (small, small_out))
+    ]
+    spread_em = Spread(at, rows, em, em_sems)
 
     def begin(l):
         spread = [Spread(at, rows, buf, spread_sems[2 * l + i]) for i, buf in enumerate((n1, n2))]
@@ -734,6 +742,8 @@
         leave(l, 0)
         if l == 0:
             begin_plane(now[C])
+            following[A].zstart()
+            following[B].zstart()
         attention(1)
         collect_one.forward(0)
         leave(l, 1)
@@ -751,13 +761,19 @@
         if l == 0:
             now[C].pforward()
             begin_plane(now[D])
+            following[C].zstart()
+        if not following:
+            swap_cotangent.wait()
+            upstream[...] = turned_cotangent[...].astype(F32) * small[3:4, :]
+            for k in range(CHUNKS):
+                em[rows.at_(k, at.mine), :] = upstream[rows.own(k), :].astype(BF16)
         second_norm(l, 1)
         collect_one.forward(3)
         second_norm(l, 2)
         second_norm(l, 3)
-        if following:
-            following[A].zstart()
-            following[B].zstart()
+        if not following:
+            for k in range(CHUNKS):
+                spread_em.start(k)
         save_x = local.start(x, middle_out)
         pending += [local.start(o, o_out), local.start(lse, lse_out)]
         save_n1.wait()
@@ -765,62 +781,68 @@
         now[C].pwait()
         for k in range(CHUNKS):
             up(l, k)
-            if k == 1:
+            if k == 1 and following:
+                begin_plane(following[A])
+            if k == 1 and not following:
                 now[D].pforward()
             if k + 1 < CHUNKS:
                 spread_two.forward(k + 1)
+        if following:
+            now[D].pforward()
+        else:
+            for k in range(CHUNKS):
+                spread_em.forward(k)
+        pending += [local.start(*pair) for pair in ((n2, n2_out), (g, g_out), (slope, slope_out))]
         save_x.wait()
         spread_two.finish()
         now[D].pwait()
+        pending += [local.start(*pair) for pair in zip(weights[l], full_outs)]
+        if not following:
+            collect_one.finish()
+            for k in range(CHUNKS):
+                spread_em.wait(k)
+            spread_em.finish()
+            pending.append(local.start(em, em_out))
+            continue
         for k in range(CHUNKS):
             down(l, k)
             if k:
                 collect_two.forward(k - 1)
-            if following:
-                if k == 0:
-                    begin_plane(following[A])
-                    following[C].zstart()
-                if k == 2:
-                    begin_plane(following[B])
+            if k == 0:
+                following[D].zstart()
+                swap_cotangent.start()
+            if k == 1:
+                begin_plane(following[B])
             if k > 1:
                 end(l, k - 2)
         collect_two.forward(CHUNKS - 1)
-        pending += [local.start(*pair) for pair in ((n2, n2_out), (g, g_out), (slope, slope_out))]
-        pending += [local.start(*pair) for pair in zip(weights[l], full_outs)]
         end(l, CHUNKS - 2)
-        if following:
-            following[A].pforward()
+        following[A].pforward()
         end(l, CHUNKS - 1)
-        if following:
-            following[D].zstart()
-        else:
-            swap_cotangent.start()
         collect_one.finish()
         collect_two.finish()
-    live = small[3:4, :]
-    mixed[...] = (x[...] * live).astype(BF16)
-    swap_cotangent.wait()
-    upstream[...] = turned_cotangent[...].astype(F32) * live
     for save in saves + pending:
         save.wait()
 
 
 def backward_kernel(n, refs):
     take = Take(refs)
-    upstream, mixed, gain_in = take(3)
+    upstream, gain_in, bias_in, small, em_in = take(5)
     ins = [take(15) for _ in range(LAYERS)]
     cosines_in, sines_in = take(2)
     mixed_out, grad_out, triple_out, triple_bias_out, exit_out, expand_out = take(6)
     expand_bias_out, shrink_out, gain_out, shift_out, bias_out = take(5)
     e, xs, wa, wb, wc, wd = take(6)
     em, ea, n2, qp, kp, vp, kt, o, g, du, lse = take(11)
-    dk, dv, dqt, dt, part, gd, ge, gt, vectors, cosines, sines = take(11)
-    turned_mixed, low_grad_own, turned_grad = take(3)
+    dk, dv, dqt, do, part, gd, ge, vectors, cosines, sines = take(10)
+    dt, gt = take(2), take(2)
+    mixed, turned_mixed, low_grad_own, turned_grad = take(4)
+    part_last, last_got, last_sems = take(), take(2), take()
     spread_sems = take(2 * LAYERS)
     one_buffers, two_buffers = take(4), take(4)
     collect_sems = take(2 * LAYERS)
-    scatter_buffers = [take(2) for _ in range(4)]
-    scatter_layers = [[take(3) for _ in range(4)] for _ in range(LAYERS)]
+    scatter_buffers = [take(2) for _ in range(5)]
+    scatter_layers = [[take(3) for _ in range(5)] for _ in range(LAYERS)]
     mixed_sems, grad_sems = take(2)
     plane, column, plane_sems, column_sems = take(4)
     local_sems = take()
@@ -856,6 +878,7 @@
 
     loads = {}
     top = LAYERS - 1
+    load_em = local.start(em_in, em)
     load_e = local.start(upstream, e)
     for name in ("d", "slope", "c", "middle", "g", "n2", "b", "q", "k", "v", "o", "lse", "a"):
         load(top, name)
@@ -884,14 +907,28 @@
         ]
         for l in range(LAYERS)
     ]
-    pieces = ((gt, triple_out, False), (ge, exit_out, True), (wd, expand_out, False), (gd, shrink_out, True))
+    def triple_columns(l, pair):
+        return [triple_out.at[l, kind, :, pl.ds(pair * LANES, LANES)] for kind in range(3)]
+
+    def pieces(l):
+        return (
+            (gt[0], triple_columns(l, 0), None),
+            (gt[1], triple_columns(l, 1), None),
+            (ge, exit_out.at[l], True),
+            (wd, expand_out.at[l], False),
+            (gd, shrink_out.at[l], True),
+        )
+
     scatters = [
         [
-            Scatter(at, grad, out.at[l], flip, *buffers, *own)
-            for (grad, out, flip), buffers, own in zip(pieces, scatter_buffers, scatter_layers[l])
+            Scatter(at, *piece, *buffers, *own)
+            for piece, buffers, own in zip(pieces(l), scatter_buffers, scatter_layers[l])
         ]
         for l in range(LAYERS)
     ]
+    collect_last = Collect(
+        at, rows, part_last, two_buffers[0], last_got[0], two_buffers[2], last_got[1], last_sems
+    )
     swap_mixed = Swap(at, mixed, turned_mixed, mixed_sems)
     swap_grads = [
         Swap(
@@ -921,7 +958,9 @@
         add(l, 5, low)
 
     def shrink_back(l, k):
-        spreads[l][0].wait(k)
+        if l < top:
+            spreads[l][0].forward(k)
+            spreads[l][0].wait(k)
         whole = rows.whole(k)
         collect = collects[l][0]
 
@@ -967,39 +1006,78 @@
             low_grad_own[rows.own(k), :] = e[rows.own(k), :].astype(BF16)
             swap_grads[k].start()
 
-    def attention_back(l, k):
-        spreads[l][1].wait(k)
+    def branch_last(k):
+        left = collect_last.left(g, k)
+
+        def outputs(j, carry):
+            span = tile(j, 256)
+            collect_last.put(k, span, dot(left, wd[span, :], NT))
+            return carry
+
+        lax.fori_loop(0, part.shape[2] // 256, outputs, 0)
+        collect_last.start(k)
+
+    def end_last(k):
+        own = rows.own(k)
+        bias = bias_in[top, 1:2, :].astype(F32)
+        hidden = xs[own, :] + (collect_last.take(k) + bias)
+        mixed[own, :] = (hidden * small[3:4, :]).astype(BF16)
+
+    def attention_back(l, pair, k):
         whole = rows.whole(k)
-        out_grad = dot(ea[whole, :], wb[...], NN)
-        low_grad = out_grad.astype(BF16)
-        product = low_grad.astype(F32) * o[whole, :].astype(F32)
+        if pair == 0:
+            spreads[l][1].wait(k)
+            do[whole, :] = dot(ea[whole, :], wb[...], NN).astype(BF16)
+        lanes = slice(pair * LANES, (pair + 1) * LANES)
+        dop = do[whole, lanes]
+        product = dop.astype(F32) * o[whole, lanes].astype(F32)
         high = product.astype(BF16)
         rest = (product - high.astype(F32)).astype(BF16)
+        for half in range(2):
+            h = 2 * pair + half
+            pick = jnp.broadcast_to(((lane() // HEAD_DIM) == half).astype(BF16), (8, LANES))
+            center = dot(pick, high, NT) + dot(pick, rest, NT)
+            qh = of_head(qp[pair, whole, :], half)
+            doh = of_head(dop, half)
+            scores = dot(kp[pair], qh, NT)
+            chances = jnp.exp2(scores - lse[h : h + 1, whole])
+            chance_grad = dot(vp[pair], doh, NT)
+            score_grad = (chances * (chance_grad - center[0:1, :])).astype(BF16)
+            dv[pair] += dot(chances.astype(BF16), doh, NN)
+            dk[pair] += dot(score_grad, qh, NN)
+            spans = slice(h * HEAD_DIM, (h + 1) * HEAD_DIM)
+            dqt[half * HEAD_DIM : (half + 1) * HEAD_DIM, :] = dot(kt[spans, :], score_grad, NN)
+        dq = dqt[...].T * SCALE
+        dt[pair][whole, :LANES] = turned(dq, cosines[whole, :], -sines[whole, :]).astype(BF16)
+
+    def pair_done(l, pair):
+        dt[pair][:, LANES : 2 * LANES] = turned(
+            dk[pair] * LN2, cosines[...], -sines[...]
+        ).astype(BF16)
+        dt[pair][:, 2 * LANES :] = dv[pair].astype(BF16)
+        weight_grad(g, dt[pair], gt[pair])
+        scatters[l][pair].pstart()
+
+    def triple_sum(l):
+        width = 2 * LANES
         for pair in range(2):
-            lanes = slice(pair * LANES, (pair + 1) * LANES)
-            dop = low_grad[:, lanes]
-            for half in range(2):
-                h = 2 * pair + half
-                pick = jnp.broadcast_to(((lane() // HEAD_DIM) == half).astype(BF16), (8, LANES))
-                center = dot(pick, high[:, lanes], NT) + dot(pick, rest[:, lanes], NT)
-                qh = of_head(qp[pair, whole, :], half)
-                doh = of_head(dop, half)
-                scores = dot(kp[pair], qh, NT)
-                chances = jnp.exp2(scores - lse[h : h + 1, whole])
-                chance_grad = dot(vp[pair], doh, NT)
-                score_grad = (chances * (chance_grad - center[0:1, :])).astype(BF16)
-                dv[pair] += dot(chances.astype(BF16), doh, NN)
-                dk[pair] += dot(score_grad, qh, NN)
-                spans = slice(h * HEAD_DIM, (h + 1) * HEAD_DIM)
-                dqt[spans, :] = dot(kt[spans, :], score_grad, NN)
-        for pair in range(2):
-            lanes = slice(pair * LANES, (pair + 1) * LANES)
-            dq = dqt[lanes, :].T * SCALE
-            dt[whole, lanes] = turned(dq, cosines[whole, :], -sines[whole, :]).astype(BF16)
+            sums = jnp.sum(dt[pair][...].astype(F32), axis=0, keepdims=True)
+            for kind in range(3):
+                start = kind * width + pair * LANES
+                vectors[8 * l + 7 : 8 * l + 8, start : start + LANES] = sums[
+                    :, kind * LANES : (kind + 1) * LANES
+                ]
 
     def projection_back(l, k):
         collect = collects[l][1]
-        left = collect.left(dt, k)
+        left = jnp.concatenate(
+            [
+                collect.left(dt[pair], k)[:, kind * LANES : (kind + 1) * LANES]
+                for kind in range(3)
+                for pair in range(2)
+            ],
+            axis=1,
+        )
 
         def outputs(j, carry):
             span = tile(j, 256)
@@ -1010,35 +1088,39 @@
         collect.start(k)
 
     load_e.wait()
+    load_em.wait()
     for k in range(CHUNKS):
-        send_branch(top, k)
-    swap_mixed.start()
+        add(top, 5, em[rows.at_(k, at.mine), :])
     for l in reversed(range(LAYERS)):
         spread_one, spread_two = spreads[l]
         collect_one, collect_two = collects[l]
-        st, se, sc, sd = scatters[l]
+        st0, st1, se, sc, sd = scatters[l]
         previous = scatters[l + 1] if l < top else None
         ready(l, "d", "slope", "c", "middle")
         for k in range(CHUNKS):
-            spread_one.forward(k)
             shrink_back(l, k)
             if k:
                 collect_one.forward(k - 1)
             if k > 1:
                 middle_step(l, k - 2)
         collect_one.forward(CHUNKS - 1)
-        spread_one.finish()
         if previous:
-            for scatter in previous[:2]:
-                scatter.psum()
-                scatter.zstart()
+            spread_one.finish()
+            previous[1].psum()
         ready(l, "g")
+        if l == top:
+            branch_last(0)
+            branch_last(1)
         weight_grad(em, g, gd)
         sd.pstart()
-        load(l, "n1")
         middle_step(l, CHUNKS - 2)
         middle_step(l, CHUNKS - 1)
-        load(l, "hidden")
+        if l == top:
+            branch_last(2)
+            branch_last(3)
+        else:
+            load(l, "hidden")
+        load(l, "n1")
         ready(l, "n2")
         weight_grad(n2, du, wd)
         sc.pstart()
@@ -1056,56 +1138,76 @@
                 copy.wait()
         spread_two.forward(0)
         spread_two.forward(1)
-        attention_back(l, 0)
+        attention_back(l, 0, 0)
         spread_two.forward(2)
         spread_two.forward(3)
         sd.pforward()
-        attention_back(l, 1)
+        if l == top:
+            collect_last.forward(0)
+            collect_last.forward(1)
+        else:
+            previous[1].zstart()
+        attention_back(l, 0, 1)
+        if l == top:
+            collect_last.forward(2)
+            collect_last.forward(3)
         sc.pforward()
-        attention_back(l, 2)
-        if previous:
-            for scatter in previous[:2]:
-                scatter.zsum()
+        attention_back(l, 0, 2)
         sd.psum()
         sd.zstart()
-        attention_back(l, 3)
+        attention_back(l, 0, 3)
         spread_two.finish()
+        weight_grad(ea, o, ge)
+        se.pstart()
+        ready(l, "n1")
+        pair_done(l, 0)
         sc.psum()
         sc.zstart()
-        width = 2 * LANES
-        for pair in range(2):
-            lanes = pl.ds(width + pair * LANES, LANES)
-            dt[:, lanes] = turned(dk[pair] * LN2, cosines[...], -sines[...]).astype(BF16)
-            dt[:, pl.ds(2 * width + pair * LANES, LANES)] = dv[pair].astype(BF16)
-        ready(l, "a", "n1")
-        weight_grad(g, dt, gt)
-        st.pstart()
+        attention_back(l, 1, 0)
+        if l == top:
+            for k in range(CHUNKS):
+                end_last(k)
+            load(l, "hidden")
+            swap_mixed.start()
+        else:
+            previous[1].zsum()
+        attention_back(l, 1, 1)
+        se.pforward()
+        st0.pforward()
+        attention_back(l, 1, 2)
+        se.psum()
+        se.zstart()
+        attention_back(l, 1, 3)
+        st0.psum()
+        st0.zstart()
+        ready(l, "a")
+        if l == top:
+            collect_last.finish()
+        pair_done(l, 1)
         for k in range(CHUNKS):
             projection_back(l, k)
             if k:
                 collect_two.forward(k - 1)
         collect_two.forward(CHUNKS - 1)
-        weight_grad(ea, o, ge)
-        se.pstart()
-        add(l, 7, dt[...])
+        triple_sum(l)
         ready(l, "hidden")
         if l:
             for name in ("d", "g", "b", "q", "k", "v", "o", "lse", "a"):
                 load(l - 1, name)
+        collect_one.finish()
         sd.zsum()
-        collect_one.finish()
         first_step(l, 0)
         first_step(l, 1)
-        st.pforward()
-        se.pforward()
+        st1.pforward()
         first_step(l, 2)
         first_step(l, 3)
         if l:
             load(l - 1, "middle")
         collect_two.finish()
-        sc.zsum()
-
-    st, se = scatters[0][:2]
+        for scatter in (sc, se, st0):
+            scatter.zsum()
+
+    last = scatters[0][1]
     plane[at.dh] = vectors[...]
 
     def plane_copy(step, slot):
@@ -1114,9 +1216,8 @@
 
     for step in range(1, n):
         plane_copy(step, at.dh).start()
-    for scatter in (st, se):
-        scatter.psum()
-        scatter.zstart()
+    last.psum()
+    last.zstart()
     for step in range(1, n):
         plane_copy(step, at.dh).wait_send()
         plane_copy(step, lax.rem(at.dh + n - step, n)).wait_recv()
@@ -1138,7 +1239,7 @@
     for index, flips in enumerate(cubes):
         column_copy(index, flips, mine).start()
     swap_mixed.wait()
-    mixed_out[...] = turned_mixed[...].astype(F32)
+    save_mixed = local.start(turned_mixed, mixed_out)
     for index, flips in enumerate(cubes):
         column_copy(index, flips, mine).wait_send()
         column_copy(index, flips, slot(*flipped(flips))).wait_recv()
@@ -1153,14 +1254,24 @@
         bias_out[l] = total[8 * l + 4 : 8 * l + 6, :]
         expand_bias_out[l : l + 1, :] = own[8 * l + 6 : 8 * l + 7, :]
         for kind in range(3):
-            triple_bias_out[l, kind : kind + 1, :] = own[
+            triple_bias_out[kind, l : l + 1, :] = own[
                 8 * l + 7 : 8 * l + 8, kind * width : (kind + 1) * width
             ]
     for k in range(CHUNKS):
         swap_grads[k].wait()
-    grad_out[...] = turned_grad[...].astype(F32)
-    for scatter in (st, se):
-        scatter.zsum()
+    save_grad = local.start(turned_grad, grad_out)
+    last.zsum()
+    save_mixed.wait()
+    save_grad.wait()
+
+
+def finish_kernel(*refs):
+    half = len(refs) // 2
+    for source, target in zip(refs[:half], refs[half:]):
+        if len(source.shape) < len(target.shape):
+            target[:, 0, :] = source[...].astype(F32)
+        else:
+            target[...] = source[...]
 
 
 def call(body, args, vmem_in, outs, vmem_out, scratch, collective_id, name, flops=0):
@@ -1214,8 +1325,8 @@
         cotangent[:, 0, :],
         clip_mask[:, None],
         positions[:, 0, :],
-        triple_weight.reshape(LAYERS, size, wide),
-        triple_bias,
+        triple_weight.transpose(0, 2, 1, 3),
+        triple_bias.transpose(1, 0, 2),
         exit_weight,
         expand_weight,
         expand_bias,
@@ -1225,10 +1336,11 @@
         branch_bias,
     ]
     outs = [
-        shape((count, depth), BF16),
         shape((count, depth), F32),
         shape((seq, LANES), F32),
         shape((seq, LANES), F32),
+        shape((8, depth), F32),
+        shape((seq, depth), BF16),
     ]
     for _ in range(LAYERS):
         outs += [shape((count, depth), F32)] * 2
@@ -1249,6 +1361,8 @@
         V((seq, LANES), F32),
         V((LAYERS, size, local), BF16),
         V((LAYERS, size, inner), BF16),
+        V((LAYERS, size, wide), BF16),
+        V((seq, depth), BF16),
     ]
     for _ in range(LAYERS):
         scratch += [V((depth, width), BF16) for width in wides]
@@ -1261,24 +1375,25 @@
     scratch += Collect.scratch(count, depth) * 2
     scratch += [Collect.SEMS] * (2 * LAYERS)
     scratch += Gather.scratch(n) * (4 * LAYERS)
+    scratch += Spread.scratch(depth)
     scratch += [DMA((CHUNKS, 3)), DMA((3,)), DMA((3,)), DMA((48,))]
     results = call(
         functools.partial(forward_kernel, n),
         args,
         tuple(range(len(args))),
         outs,
-        (0, 1),
+        (0,),
         scratch,
         1,
         "forward",
     )
-    mixed, upstream, cosines, sines = results[:4]
-    args = [upstream, mixed, norm_gain, *results[4:], cosines, sines]
+    upstream, cosines, sines, small, em = results[:5]
+    args = [upstream, norm_gain, branch_bias, small, em, *results[5:], cosines, sines]
     outs = [
-        shape((count, depth), F32),
-        shape((count, depth), F32),
-        shape((LAYERS, size, wide), F32),
-        shape(triple_bias.shape, F32),
+        shape((count, depth), BF16),
+        shape((count, depth), BF16),
+        shape((LAYERS, 3, size, local), F32),
+        shape((3, LAYERS, local), F32),
         shape(exit_weight.shape, F32),
         shape(expand_weight.shape, F32),
         shape(expand_bias.shape, F32),
@@ -1295,17 +1410,20 @@
     scratch += [V((seq, inner), BF16)] * 2
     scratch += [V((8, seq), F32)]
     scratch += [V(pair_shape, F32)] * 2
-    scratch += [V((local, 4 * R), F32), V((seq, wide), BF16), V((CHUNKS, 2 * R, depth), F32)]
-    scratch += [V((depth, inner), BF16), V((depth, local), BF16), V((depth, wide), BF16)]
+    scratch += [V((LANES, 4 * R), F32), V((seq, local), BF16), V((CHUNKS, 2 * R, depth), F32)]
+    scratch += [V((depth, inner), BF16), V((depth, local), BF16)]
     scratch += [V((8 * LAYERS, depth), F32), V((seq, LANES), F32), V((seq, LANES), F32)]
-    scratch += [V((count, depth), BF16)] * 3
+    scratch += [V((seq, 3 * LANES), BF16)] * 2 + [V((depth, 3 * LANES), BF16)] * 2
+    scratch += [V((count, depth), BF16)] * 4
+    scratch += [V((CHUNKS, 2 * R, depth), F32)] + Collect.scratch(count, depth)[1::2] + [Collect.SEMS]
     scratch += Spread.scratch(depth) * (2 * LAYERS)
     scratch += Collect.scratch(count, depth) * 2
     scratch += [Collect.SEMS] * (2 * LAYERS)
-    for width in wides:
+    widths = (3 * LANES, 3 * LANES, local, inner, inner)
+    for width in widths:
         scratch += Scatter.scratch(n, depth, width)
     for _ in range(LAYERS):
-        for width in wides:
+        for width in widths:
             scratch += Scatter.layer_scratch(n, depth, width)
     scratch += [DMA((3,)), DMA((CHUNKS, 3))]
     scratch += [V((n, 8 * LAYERS, depth), F32), V((8, 8 * LAYERS, depth), F32)]
@@ -1313,18 +1431,22 @@
     results = call(
         functools.partial(backward_kernel, n),
         args,
-        (1, 2),
+        (1, 2, 3),
         outs,
-        tuple(range(len(outs))),
+        tuple(range(2, len(outs))),
         scratch,
         2,
         "backward",
     )
-    mixed, grad, triple_total, *others = results
+    outs = [shape((count, 1, depth), F32)] * 2 + [shape(r.shape, F32) for r in results[2:]]
+    mixed, grad, triple_total, bias_total, *others = pl.pallas_call(
+        finish_kernel, out_shape=outs, name="finish"
+    )(*results)
     return (
-        mixed[:, None, :],
-        grad[:, None, :],
-        triple_total.reshape(triple_weight.shape),
+        mixed,
+        grad,
+        triple_total.transpose(0, 2, 1, 3),
+        bias_total.transpose(1, 0, 2),
         *others,
     )
 

time: 468 us -> 451 us (0.964)
  local copies, waits for them, and re-layouts: 17.3 us -> 1.32 us
    unnamed x34 -> x1, local copies, waits for them, and re-layouts: 16.1 us -> 1.32 us
    pallas_call x2, Pallas kernels: 442 us -> 435 us  [call(): pl.pallas_call(kernel, out_shape=outs, in_specs=in_specs, out_specs=out_s...]
    pallas_call x0 -> x1, Pallas kernels: none -> 4.83 us  [shards(): pl.pallas_call(finish_kernel, out_shape=outs, name='finish')(*results)]
where the time goes in v1:
time: 451 us; the launch traced here: 443 us
  Pallas kernels  440 us (98%)
    pallas_call x2, Pallas kernels, call(): pl.pallas_call(kernel, out_shape=outs, in_specs=in_specs, out_specs=out_s...  435 us

profile of v1, /device:TPU:1, one launch (start us, length us, event | category | flops | bytes accessed | tf_op | source)
XLA Modules:
  0.0 442.7 jit_solution(4812203466448164473)
XLA Ops:
  1.3 1.3 copy.26
  2.6 205.2 %forward.1 = (f32[256,1024]{1,0:T(8,128)}, f32[1024,128]{1,0:T(8,128)}, f32[1024,128]{1,0:T(8,128)}, f32[8,1024]{1,0:T(8,128)}, bf16[1024,1024]{1,0:T(8,128)(2,1...) custom-call(bf16[256,1024]{1,0:T(8,128)(2,1)} %bitcast.11, ...), custom_call_target="tpu_custom_call" | custom-call | tf_op jit(solution)/shard_map/forward/pallas_call | solution.py:1283
  207.8 229.6 %backward.1 = (bf16[256,1024]{1,0:T(8,128)(2,1)}, bf16[256,1024]{1,0:T(8,128)(2,1)}, f32[2,3,128,256]{3,2,1,0:T(8,128)}, f32[3,2,256]{2,1,0:T(2,128)}, f32[2,256...) custom-call(f32[256,1024]{1,0:T(8,128)} %get-tuple-element.68.refs_0, ...), custom_call_target="tpu_custom_call" | custom-call | tf_op jit(solution)/shard_map/backward/pallas_call | solution.py:1283
  437.5 4.8 %finish.1 = (f32[256,1,1024]{2,1,0:T(1,128)}, f32[256,1,1024]{2,1,0:T(1,128)}, f32[2,3,128,256]{3,2,1,0:T(8,128)}, f32[3,2,256]{2,1,0:T(2,128)}, f32[2,256,128]{...) custom-call(bf16[256,1024]{1,0:T(8,128)(2,1)} %get-tuple-element.103, ...), custom_call_target="tpu_custom_call" | custom-call | tf_op jit(solution)/shard_map/finish/pallas_call | solution.py:1442

commit v2 on v1

--- a/solution.py
+++ b/solution.py
@@ -654,7 +654,7 @@
             collect.put(k, span, dot(left, wb[span, :], NT))
             return carry
 
-        lax.fori_loop(0, part.shape[2] // 256, columns, 0)
+        lax.fori_loop(0, part.shape[2] // 256, columns, 0, unroll=True)
         collect.start(k)
 
     def second_norm(l, k):
@@ -676,7 +676,7 @@
             slope[whole, span] = grade.astype(BF16)
             return carry
 
-        lax.fori_loop(0, wc.shape[1] // 256, columns, 0)
+        lax.fori_loop(0, wc.shape[1] // 256, columns, 0, unroll=True)
 
     def down(l, k):
         wd, collect = weights[l][3], stages[l][3]
@@ -687,7 +687,7 @@
             collect.put(k, span, dot(left, wd[span, :], NT))
             return carry
 
-        lax.fori_loop(0, part.shape[2] // 256, outputs, 0)
+        lax.fori_loop(0, part.shape[2] // 256, outputs, 0, unroll=True)
         collect.start(k)
 
     def end(l, k):
@@ -949,7 +949,7 @@
             out[span, :] = dot(left[:, span], right[...], TN).astype(BF16)
             return carry
 
-        lax.fori_loop(0, left.shape[1] // 256, block, 0)
+        lax.fori_loop(0, left.shape[1] // 256, block, 0, unroll=True)
 
     def send_branch(l, k):
         low = e[rows.own(k), :].astype(BF16)
@@ -970,7 +970,7 @@
             du[whole, span] = (active_grad * du[whole, span].astype(F32)).astype(BF16)
             return carry
 
-        lax.fori_loop(0, wd.shape[1] // 256, columns, 0)
+        lax.fori_loop(0, wd.shape[1] // 256, columns, 0, unroll=True)
         add(l, 6, du[whole, :])
         left = collect.left(du, k)
 
@@ -979,7 +979,7 @@
             collect.put(k, span, dot(left, wc[span, :], NT))
             return carry
 
-        lax.fori_loop(0, part.shape[2] // 256, outputs, 0)
+        lax.fori_loop(0, part.shape[2] // 256, outputs, 0, unroll=True)
         collect.start(k)
 
     def norm_step(l, k, which):
@@ -1014,7 +1014,7 @@
             collect_last.put(k, span, dot(left, wd[span, :], NT))
             return carry
 
-        lax.fori_loop(0, part.shape[2] // 256, outputs, 0)
+        lax.fori_loop(0, part.shape[2] // 256, outputs, 0, unroll=True)
         collect_last.start(k)
 
     def end_last(k):
@@ -1084,7 +1084,7 @@
             collect.put(k, span, dot(left, wa[span, :], NT))
             return carry
 
-        lax.fori_loop(0, part.shape[2] // 256, outputs, 0)
+        lax.fori_loop(0, part.shape[2] // 256, outputs, 0, unroll=True)
         collect.start(k)
 
     load_e.wait()

time: 451 us -> 437 us (0.969)
  Pallas kernels: 440 us -> 428 us
    pallas_call x2, Pallas kernels: 435 us -> 423 us  [call(): pl.pallas_call(kernel, out_shape=outs, in_specs=in_specs, out_specs=out_s...]
where the time goes in v2:
time: 437 us; the launch traced here: 431 us
  Pallas kernels  428 us (98%)
    pallas_call x2, Pallas kernels, call(): pl.pallas_call(kernel, out_shape=outs, in_specs=in_specs, out_specs=out_s...  423 us

profile of v2, /device:TPU:1, one launch (start us, length us, event | category | flops | bytes accessed | tf_op | source)
XLA Modules:
  0.0 430.9 jit_solution(2701773311656139634)
XLA Ops:
  1.3 1.3 copy.26
  2.6 201.9 %forward.1 = (f32[256,1024]{1,0:T(8,128)}, f32[1024,128]{1,0:T(8,128)}, f32[1024,128]{1,0:T(8,128)}, f32[8,1024]{1,0:T(8,128)}, bf16[1024,1024]{1,0:T(8,128)(2,1...) custom-call(bf16[256,1024]{1,0:T(8,128)(2,1)} %bitcast.11, ...), custom_call_target="tpu_custom_call" | custom-call | tf_op jit(solution)/shard_map/forward/pallas_call | solution.py:1283
  204.5 221.3 %backward.1 = (bf16[256,1024]{1,0:T(8,128)(2,1)}, bf16[256,1024]{1,0:T(8,128)(2,1)}, f32[2,3,128,256]{3,2,1,0:T(8,128)}, f32[3,2,256]{2,1,0:T(2,128)}, f32[2,256...) custom-call(f32[256,1024]{1,0:T(8,128)} %get-tuple-element.68.refs_0, ...), custom_call_target="tpu_custom_call" | custom-call | tf_op jit(solution)/shard_map/backward/pallas_call | solution.py:1283
  425.8 4.8 %finish.1 = (f32[256,1,1024]{2,1,0:T(1,128)}, f32[256,1,1024]{2,1,0:T(1,128)}, f32[2,3,128,256]{3,2,1,0:T(8,128)}, f32[3,2,256]{2,1,0:T(2,128)}, f32[2,256,128]{...) custom-call(bf16[256,1024]{1,0:T(8,128)(2,1)} %get-tuple-element.103, ...), custom_call_target="tpu_custom_call" | custom-call | tf_op jit(solution)/shard_map/finish/pallas_call | solution.py:1442

commit v3 on v2

--- a/solution.py
+++ b/solution.py
@@ -24,7 +24,7 @@
 MESH = pl.DeviceIdType.MESH
 ANY = pl.BlockSpec(memory_space=pl.ANY)
 VMEM = pl.BlockSpec(memory_space=pltpu.VMEM)
-VMEM_LIMIT = 59 * 2**20
+VMEM_LIMIT = 60 * 2**20
 
 
 def dot(left, right, dims):
@@ -761,7 +761,6 @@
         if l == 0:
             now[C].pforward()
             begin_plane(now[D])
-            following[C].zstart()
         if not following:
             swap_cotangent.wait()
             upstream[...] = turned_cotangent[...].astype(F32) * small[3:4, :]
@@ -771,7 +770,9 @@
         collect_one.forward(3)
         second_norm(l, 2)
         second_norm(l, 3)
-        if not following:
+        if following:
+            following[C].zstart()
+        else:
             for k in range(CHUNKS):
                 spread_em.start(k)
         save_x = local.start(x, middle_out)
@@ -808,9 +809,6 @@
             down(l, k)
             if k:
                 collect_two.forward(k - 1)
-            if k == 0:
-                following[D].zstart()
-                swap_cotangent.start()
             if k == 1:
                 begin_plane(following[B])
             if k > 1:
@@ -819,6 +817,8 @@
         end(l, CHUNKS - 2)
         following[A].pforward()
         end(l, CHUNKS - 1)
+        following[D].zstart()
+        swap_cotangent.start()
         collect_one.finish()
         collect_two.finish()
     for save in saves + pending:
@@ -1033,6 +1033,7 @@
         product = dop.astype(F32) * o[whole, lanes].astype(F32)
         high = product.astype(BF16)
         rest = (product - high.astype(F32)).astype(BF16)
+        kept = []
         for half in range(2):
             h = 2 * pair + half
             pick = jnp.broadcast_to(((lane() // HEAD_DIM) == half).astype(BF16), (8, LANES))
@@ -1043,10 +1044,14 @@
             chances = jnp.exp2(scores - lse[h : h + 1, whole])
             chance_grad = dot(vp[pair], doh, NT)
             score_grad = (chances * (chance_grad - center[0:1, :])).astype(BF16)
-            dv[pair] += dot(chances.astype(BF16), doh, NN)
-            dk[pair] += dot(score_grad, qh, NN)
+            kept.append((chances.astype(BF16), doh, score_grad, qh))
             spans = slice(h * HEAD_DIM, (h + 1) * HEAD_DIM)
             dqt[half * HEAD_DIM : (half + 1) * HEAD_DIM, :] = dot(kt[spans, :], score_grad, NN)
+        low_chances, dohs, score_grads, qhs = [
+            jnp.concatenate(two, axis=axis) for two, axis in zip(zip(*kept), (1, 0, 1, 0))
+        ]
+        dv[pair] += dot(low_chances, dohs, NN)
+        dk[pair] += dot(score_grads, qhs, NN)
         dq = dqt[...].T * SCALE
         dt[pair][whole, :LANES] = turned(dq, cosines[whole, :], -sines[whole, :]).astype(BF16)
 

time: 437 us -> 432 us (0.989)
  Pallas kernels: 428 us -> 422 us
    pallas_call x2, Pallas kernels: 423 us -> 418 us  [call(): pl.pallas_call(kernel, out_shape=outs, in_specs=in_specs, out_specs=out_s...]
where the time goes in v3:
time: 432 us; the launch traced here: 425 us
  Pallas kernels  422 us (98%)
    pallas_call x2, Pallas kernels, call(): pl.pallas_call(kernel, out_shape=outs, in_specs=in_specs, out_specs=out_s...  418 us

profile of v3, /device:TPU:1, one launch (start us, length us, event | category | flops | bytes accessed | tf_op | source)
XLA Modules:
  0.0 425.3 jit_solution(7254916638402749220)
XLA Ops:
  1.3 1.3 copy.26
  2.6 193.6 %forward.1 = (f32[256,1024]{1,0:T(8,128)}, f32[1024,128]{1,0:T(8,128)}, f32[1024,128]{1,0:T(8,128)}, f32[8,1024]{1,0:T(8,128)}, bf16[1024,1024]{1,0:T(8,128)(2,1...) custom-call(bf16[256,1024]{1,0:T(8,128)(2,1)} %bitcast.11, ...), custom_call_target="tpu_custom_call" | custom-call | tf_op jit(solution)/shard_map/forward/pallas_call | solution.py:1288
  196.2 224.0 %backward.1 = (bf16[256,1024]{1,0:T(8,128)(2,1)}, bf16[256,1024]{1,0:T(8,128)(2,1)}, f32[2,3,128,256]{3,2,1,0:T(8,128)}, f32[3,2,256]{2,1,0:T(2,128)}, f32[2,256...) custom-call(f32[256,1024]{1,0:T(8,128)} %get-tuple-element.68.refs_0, ...), custom_call_target="tpu_custom_call" | custom-call | tf_op jit(solution)/shard_map/backward/pallas_call | solution.py:1288
  420.2 4.8 %finish.1 = (f32[256,1,1024]{2,1,0:T(1,128)}, f32[256,1,1024]{2,1,0:T(1,128)}, f32[2,3,128,256]{3,2,1,0:T(8,128)}, f32[3,2,256]{2,1,0:T(2,128)}, f32[2,256,128]{...) custom-call(bf16[256,1024]{1,0:T(8,128)(2,1)} %get-tuple-element.103, ...), custom_call_target="tpu_custom_call" | custom-call | tf_op jit(solution)/shard_map/finish/pallas_call | solution.py:1447
